TPU v7x, 128 devices: a whole 4x4x4 slice. The times are simulated.
128 devices in a mesh: mp: 4 (over x_hi, core), lat: 32 (over y, z, x_lo).
Axes of the slice: x: 4 (x_hi: 2, x_lo: 2; x = x_hi * 2 + x_lo), y: 4, z: 4, core: 2. Of those that a mesh axis runs over, the one named last changes fastest.
Arguments:
- resid_in: bfloat16 [1024, 2304], P('lat'), may hold values from -6 to 6
- layer_terms: bfloat16 [4, 1024, 2304], P('mp', 'lat'), may hold values from -4 to 4
- dec_bias: float32 [2304], replicated, may hold values from -3 to 3
- enc_weight: bfloat16 [2304, 65536], P(None, ('mp', 'lat')), may hold values from -0.125 to 0.125
- enc_bias: float32 [65536], P(('mp', 'lat')), may hold values from -4.5 to -2
- dec_weight: bfloat16 [65536, 2304], P(('mp', 'lat')), may hold values from -0.25 to 0.25
- first_moment: float32 [2304, 65536], P(None, ('mp', 'lat')), may hold values from -0.6 to 0.6
- second_moment: float32 [2304, 65536], P(None, ('mp', 'lat')), may hold values from 0.002 to 0.3
Outputs:
- enc_weight_new: bfloat16 [2304, 65536], P(None, ('mp', 'lat'))
- first_moment_new: float32 [2304, 65536], P(None, ('mp', 'lat'))
- second_moment_new: float32 [2304, 65536], P(None, ('mp', 'lat'))
- recon_error: bfloat16 [1024, 2304], P(('mp', 'lat'))
All inputs are finite; a program needn't handle non-finite values.
Results may differ from a plain program's by a relative error of at most 0.02.
The roundings to bfloat16 on the way count: a program that leaves them out, or rounds other values in their place, can miss the bound.
Values may be sent and summed in bfloat16 or wider, within the bound.
A program may use at most 128 MiB of HBM per device.

v0:
```python
import jax
import jax.numpy as jnp
from jax import lax
from jax.experimental import pallas as pl
from jax.experimental.pallas import tpu as pltpu
from jax.sharding import PartitionSpec as P

MESH = pl.DeviceIdType.MESH
STEP = 10
l1_coeff = 5.0
loss_norm = 32.0
beta_one = 0.9
beta_two = 0.95
learn_rate = 0.001
adam_eps = 1e-08

D = 2304
HALF = D // 2
GROUP = HALF // 3
PARTS = 3
LAT_DEV = 512
ROWS = 1024
BLOCK = 16
TILE = 256
ORDER = ((2, 1, 0), (0, 2, 1), (1, 0, 2))


def exchange_kernel(
    resid, terms, dec_bias, enc_weight, enc_bias, dec_weight,
    kept_out,
    cen, err, cen_t, weight, dec, dec_t, norms, codes, cross_send, cross_recv, part_sum,
    a_send, a_recv, b_send, b_recv, c_send, c_recv, plane_sum, slopes, half_sum,
    term_in, resid_in, bias_in, enc_bias_in, own_cen, error_rows,
    send_sems, recv_sems, local_sems, ready,
):
    m = lax.axis_index("mp")
    lat = lax.axis_index("lat")
    core = lax.rem(m, 2)
    yz = lax.div(lat, 2)
    x = lax.div(m, 2) * 2 + lax.rem(lat, 2)
    pos = (x, lax.div(yz, 4), lax.rem(yz, 4))

    def device(at, on_core):
        return (lax.div(at[0], 2) * 2 + on_core, (at[1] * 4 + at[2]) * 2 + lax.rem(at[0], 2))

    def along(axis, k):
        return lax.rem(pos[axis] + k, 4)

    def peer(axis, k):
        at = list(pos)
        at[axis] = along(axis, k)
        return device(at, core)

    other = device(pos, 1 - core)
    g0 = core * PARTS

    count = [0, 0]
    sent = []

    def remote(src, dst, to):
        i = count[0]
        count[0] += 1
        copy = pltpu.make_async_remote_copy(
            src_ref=src, dst_ref=dst, send_sem=send_sems.at[i], recv_sem=recv_sems.at[i],
            device_id=to, device_id_type=MESH,
        )
        copy.start()
        sent.append(copy)
        return copy

    def local(src, dst):
        i = count[1]
        count[1] += 1
        copy = pltpu.make_async_copy(src, dst, local_sems.at[i])
        copy.start()
        return copy

    rows16 = pl.ds(pl.multiple_of(lax.div(m, 2) * BLOCK, BLOCK), BLOCK)
    half = pl.ds(pl.multiple_of(core * HALF, 128), HALF)
    early = [
        local(terms.at[0, rows16, half], term_in.at[0]),
        local(resid.at[rows16, half], resid_in),
        local(dec_bias, bias_in),
        local(enc_bias, enc_bias_in),
    ]
    load_dec = [local(dec_weight.at[:, pl.ds(h * HALF, HALF)], dec.at[h]) for h in range(2)]
    load_weight = local(enc_weight, weight)

    barrier = pltpu.get_barrier_semaphore()
    greet = [other, device((lax.rem(x + 2, 4), pos[1], pos[2]), 1 - core)]
    greet += [peer(axis, k) for axis in range(3) for k in (1, 2, 3)]
    for to in greet:
        pl.semaphore_signal(barrier, inc=1, device_id=to, device_id_type=MESH)
    pl.semaphore_wait(barrier, len(greet))
    for to in greet[2:]:
        pl.semaphore_signal(ready, inc=1, device_id=to, device_id_type=MESH)

    moves = []
    for k in (1, 2, 3):
        mt = lax.rem(m + k, 4)
        moves.append(
            remote(
                terms.at[
                    0,
                    pl.ds(pl.multiple_of(lax.div(mt, 2) * BLOCK, BLOCK), BLOCK),
                    pl.ds(pl.multiple_of(lax.rem(mt, 2) * HALF, 128), HALF),
                ],
                term_in.at[k],
                (mt, lat),
            )
        )
    for copy in early:
        copy.wait()
    for copy in moves:
        copy.wait_recv()
    total = term_in[0].astype(jnp.float32)
    for k in (1, 2, 3):
        total = total + term_in[k].astype(jnp.float32)
    bias = bias_in[...].reshape(1, D)
    bias = jnp.where(core == 0, bias[:, :HALF], bias[:, HALF:])
    own = (resid_in[...].astype(jnp.float32) + total - bias).astype(jnp.bfloat16)
    for p in range(PARTS):
        own_cen[p] = own[:, p * GROUP : (p + 1) * GROUP]

    def place(sel):
        return (
            pl.ds(*sel[0]),
            pl.ds(*sel[1]),
            pl.ds(pl.multiple_of(sel[2][0] * BLOCK, BLOCK), sel[2][1] * BLOCK),
        )

    def only(base, axis, start, size):
        sel = list(base)
        sel[axis] = (start, size)
        return sel

    own_sel = [(pos[0], 1), (pos[1], 1), (pos[2], 1)]
    full = [(0, 4), (0, 4), (0, 4)]
    ROUTE = ((0,), (3,))
    STRAIGHT = (1, 2)
    STEPS = (0, 1, 3, 2)

    def plane(p, k_last, k_second):
        sel = only(full, ORDER[p][2], along(ORDER[p][2], k_last), 1)
        return only(sel, ORDER[p][1], along(ORDER[p][1], k_second), 1)

    def across_plane(p, q, r):
        at = list(pos)
        at[ORDER[p][0]] = along(ORDER[p][0], q)
        at[ORDER[p][1]] = along(ORDER[p][1], r)
        return device(at, core)

    def gather(buf, blocks, fill_one, fill_two):
        def at(p, sel):
            return buf.at[(g0 + p,) + place(sel)]

        def share(p, sel, to):
            return remote(at(p, sel), at(p, sel), to)

        for p in range(PARTS):
            buf[(g0 + p,) + place(own_sel)] = blocks[p][None, None]
        across = []
        first = [{} for _ in range(PARTS)]
        three = [[{}, {}, {}] for _ in range(PARTS)]
        four = [[{}, {}] for _ in range(PARTS)]

        def arrived(p, r):
            for q in STEPS:
                if q or r:
                    first[p][q, (4 - r) % 4].wait_recv()

        def to_neighbours(p, r):
            for way, k in ((0, 1), (1, 3)):
                three[p][way][r] = share(p, plane(p, 0, r), peer(ORDER[p][2], k))
            if r in STRAIGHT:
                three[p][2][r] = share(p, plane(p, 0, r), peer(ORDER[p][2], 2))

        def onward(p, way, r):
            k = (1, 3)[way]
            three[p][way][r].wait_recv()
            four[p][way][r] = share(p, plane(p, 4 - k, r), peer(ORDER[p][2], k))

        def over(p, k):
            sel = only(full, ORDER[p][2], along(ORDER[p][2], k), 1)
            across.append(share(p, sel, other))

        for r in STEPS:
            for p in range(PARTS):
                for q in STEPS:
                    if q or r:
                        first[p][q, r] = share(p, own_sel, across_plane(p, q, r))
        fill_one()
        for r in (0, 3, 1):
            for p in range(PARTS):
                arrived(p, r)
                to_neighbours(p, r)
        for p in range(PARTS):
            onward(p, 0, 0)
        for p in range(PARTS):
            arrived(p, 2)
            to_neighbours(p, 2)
            over(p, 0)
        fill_two()
        for p in range(PARTS):
            onward(p, 1, 3)
        for p in range(PARTS):
            three[p][0][3].wait_recv()
            three[p][1][0].wait_recv()
            for r in STRAIGHT:
                for way in range(2):
                    three[p][way][r].wait_recv()
            over(p, 1)
            over(p, 3)
        for p in range(PARTS):
            for r, copy in ((0, four[p][0][0]), (1, three[p][2][1]), (3, four[p][1][3]), (2, three[p][2][2])):
                copy.wait_recv()
                across.append(share(p, plane(p, 2, r), other))
        return across

    def nothing():
        pass

    def turn_dec():
        for copy in load_dec:
            copy.wait()

        @pl.loop(0, 2)
        def _(h):
            for q in range(PARTS):
                dec_t[pl.ds(pl.multiple_of(h * HALF + q * GROUP, 128), GROUP), :] = dec[
                    h, :, q * GROUP : (q + 1) * GROUP
                ].T

        norms[...] = jnp.zeros_like(norms)

        @pl.loop(0, 9)
        def _(r):
            rows = dec_t[pl.ds(pl.multiple_of(r * 256, 256), 256), :].astype(jnp.float32)
            norms[...] += jnp.sum(rows * rows, axis=0, keepdims=True)

        norms[...] = jnp.sqrt(norms[...]) * (l1_coeff / loss_norm)

    def wide(buf, t, of_core):
        return jnp.concatenate(
            [buf[of_core * PARTS + p, t].reshape(TILE, GROUP) for p in range(PARTS)], axis=1
        )

    def half_rows(of_core):
        return pl.ds(pl.multiple_of(of_core * HALF, 128), HALF)

    def product(buf, matrix, across, use):
        @pl.loop(0, ROWS // TILE)
        def _(t):
            half_sum[t] = jnp.dot(
                wide(buf, t, core), matrix[half_rows(core), :], preferred_element_type=jnp.float32
            )

        for copy in across:
            copy.wait_recv()
        for t in range(ROWS // TILE):
            use(
                t,
                half_sum[t]
                + jnp.dot(
                    wide(buf, t, 1 - core),
                    matrix[half_rows(1 - core), :],
                    preferred_element_type=jnp.float32,
                ),
            )

    pl.semaphore_wait(ready, len(greet) - 2)
    across = gather(cen, [own_cen[p] for p in range(PARTS)], nothing, turn_dec)
    load_weight.wait()
    keep_weight = local(weight, kept_out.at[pl.ds(D, D), pl.ds(LAT_DEV, LAT_DEV)])
    crossing = []

    def encode(t, pre):
        codes[t] = jnp.maximum(pre + enc_bias_in[...], 0.0).astype(jnp.bfloat16)
        made = jnp.dot(codes[t], dec[1 - core], preferred_element_type=jnp.float32)
        for p in range(PARTS):
            cross_send[p, t] = (
                made[:, p * GROUP : (p + 1) * GROUP].astype(jnp.bfloat16).reshape(4, 64, GROUP)
            )
        crossing.append(remote(cross_send.at[:, t], cross_recv.at[:, t], other))

    product(cen, weight, across, encode)

    @pl.loop(0, ROWS // TILE)
    def _(t):
        made = jnp.dot(codes[t], dec[core], preferred_element_type=jnp.float32)
        for p in range(PARTS):
            part_sum[p, t] = made[:, p * GROUP : (p + 1) * GROUP].reshape(4, 64, GROUP)

    for copy in crossing:
        copy.wait_recv()

    def here(p, sel):
        where = (p,) + place(sel)
        value = part_sum[where] + cross_recv[where].astype(jnp.float32)
        return value.reshape(-1, GROUP)

    def turn_centered(first, last):
        @pl.loop(0, ROWS // TILE)
        def _(t):
            for g in range(first, last):
                cen_t[g * GROUP : (g + 1) * GROUP, pl.ds(pl.multiple_of(t * TILE, TILE), TILE)] = (
                    cen[g, t].reshape(TILE, GROUP).T
                )

    step_a = [{} for _ in range(PARTS)]
    step_b = [[{}, {}] for _ in range(PARTS)]

    def to_far(p, r, k):
        a_send[p, r] = here(p, plane(p, 2, r)).astype(jnp.bfloat16)
        step_a[p][r] = remote(a_send.at[p, r], a_recv.at[p, r], peer(ORDER[p][2], k))

    def to_owner(p, way, r):
        k = (1, 3)[way]
        value = here(p, plane(p, k, r))
        if r in ROUTE[way]:
            step_a[p][r].wait_recv()
            value = value + a_recv[p, r].astype(jnp.float32)
        b_send[p, way, r] = value.astype(jnp.bfloat16)
        step_b[p][way][r] = remote(b_send.at[p, way, r], b_recv.at[p, way, r], peer(ORDER[p][2], k))

    for way, k in ((0, 1), (1, 3)):
        for r in ROUTE[way]:
            for p in range(PARTS):
                to_far(p, r, k)
    for r in (2, 1):
        for p in range(PARTS):
            to_far(p, r, 2)
            for way in range(2):
                to_owner(p, way, r)
    for way in range(2):
        for r in ROUTE[1 - way]:
            for p in range(PARTS):
                to_owner(p, way, r)
    for way in range(2):
        for r in ROUTE[way]:
            for p in range(PARTS):
                to_owner(p, way, r)
    turn_centered(0, 4)
    step_c = [{} for _ in range(PARTS)]
    for r in (2, 1, 3, 0):
        for p in range(PARTS):
            value = here(p, plane(p, 0, r))
            if r in STRAIGHT:
                step_a[p][r].wait_recv()
                value = value + a_recv[p, r].astype(jnp.float32)
            for way in range(2):
                step_b[p][way][r].wait_recv()
                value = value + b_recv[p, way, r].astype(jnp.float32)
            c_send[p, r] = value.astype(jnp.bfloat16).reshape(4, BLOCK, GROUP)
            if r == 0:
                plane_sum[p] = value.reshape(4, BLOCK, GROUP)
            for q in (2, 1, 3, 0):
                if q or r:
                    step_c[p][q, r] = remote(
                        c_send.at[p, r, along(ORDER[p][0], q)], c_recv.at[p, r, q], across_plane(p, q, r)
                    )
    kept = []
    for p in range(PARTS):
        value = plane_sum[p, pos[ORDER[p][0]]]
        for r in (2, 1, 3, 0):
            for q in STEPS:
                if q or r:
                    step_c[p][q, r].wait_recv()
                    value = value + c_recv[p, r, q].astype(jnp.float32)
        kept.append((value - own_cen[p].astype(jnp.float32)).astype(jnp.bfloat16))

    put = [keep_weight]

    def last_turn():
        turn_centered(4, 6)
        put.append(local(cen_t, kept_out.at[pl.ds(0, D)]))

    across = gather(err, kept, nothing, last_turn)

    def slope_of(t, back):
        slope = jnp.where(
            codes[t].astype(jnp.float32) > 0.0, back * (2.0 / loss_norm) + norms[...], 0.0
        )
        slopes[t * TILE : (t + 1) * TILE, :] = slope.astype(jnp.bfloat16)
        put.append(
            local(
                slopes.at[pl.ds(t * TILE, TILE)],
                kept_out.at[pl.ds(D + t * TILE, TILE), pl.ds(0, LAT_DEV)],
            )
        )

    product(err, dec_t, across, slope_of)
    row = (m * 32 + lat) * 8
    holder = lax.div(row, 32)
    hx = lax.div(lax.rem(row, 32), BLOCK) * 2 + lax.rem(holder, 2)
    hyz = lax.div(holder, 2)
    hz = pl.ds(pl.multiple_of(lax.rem(hyz, 4) * BLOCK, BLOCK), BLOCK)
    upper = lax.rem(row, BLOCK) > 0
    for g in range(2 * PARTS):
        rows = err[g, hx, lax.div(hyz, 4), hz, :].astype(jnp.float32)
        rows = jnp.where(upper, rows[8:], rows[:8])
        error_rows[:, g * GROUP : (g + 1) * GROUP] = jnp.concatenate([rows, rows]).astype(jnp.bfloat16)
    for i in range(3):
        put.append(
            local(
                error_rows.at[:, pl.ds(i * 768, 768)],
                kept_out.at[pl.ds(2 * D + i * BLOCK, BLOCK), pl.ds(0, 768)],
            )
        )
    for copy in put:
        copy.wait()
    for copy in sent:
        copy.wait_send()


N_REMOTE = 3 + 2 * PARTS * (15 + 10 + 2 + 7) + 4 + PARTS * (4 + 8 + 15)
N_LOCAL = 4 + 2 + 1 + 1 + 1 + 4 + 3
KEPT = 8192


def exchange(resid, terms, dec_bias, enc_weight, enc_bias, dec_weight):
    bf16, f32 = jnp.bfloat16, jnp.float32
    anywhere = pl.BlockSpec(memory_space=pl.ANY)
    hbm = pl.BlockSpec(memory_space=pltpu.HBM)
    return pl.pallas_call(
        exchange_kernel,
        out_shape=jax.ShapeDtypeStruct((KEPT, ROWS), bf16),
        in_specs=[hbm] * 6,
        out_specs=anywhere,
        scratch_shapes=[
            pltpu.VMEM((6, 4, 4, 64, GROUP), bf16),
            pltpu.VMEM((6, 4, 4, 64, GROUP), bf16),
            pltpu.VMEM((D, ROWS), bf16),
            pltpu.VMEM((D, LAT_DEV), bf16),
            pltpu.VMEM((2, LAT_DEV, HALF), bf16),
            pltpu.VMEM((D, LAT_DEV), bf16),
            pltpu.VMEM((1, LAT_DEV), f32),
            pltpu.VMEM((4, TILE, LAT_DEV), bf16),
            pltpu.VMEM((PARTS, 4, 4, 64, GROUP), bf16),
            pltpu.VMEM((PARTS, 4, 4, 64, GROUP), bf16),
            pltpu.VMEM((PARTS, 4, 4, 64, GROUP), f32),
            pltpu.VMEM((PARTS, 4, 64, GROUP), bf16),
            pltpu.VMEM((PARTS, 4, 64, GROUP), bf16),
            pltpu.VMEM((PARTS, 2, 4, 64, GROUP), bf16),
            pltpu.VMEM((PARTS, 2, 4, 64, GROUP), bf16),
            pltpu.VMEM((PARTS, 4, 4, BLOCK, GROUP), bf16),
            pltpu.VMEM((PARTS, 4, 4, BLOCK, GROUP), bf16),
            pltpu.VMEM((PARTS, 4, BLOCK, GROUP), f32),
            pltpu.VMEM((ROWS, LAT_DEV), bf16),
            pltpu.VMEM((4, TILE, LAT_DEV), f32),
            pltpu.VMEM((4, BLOCK, HALF), bf16),
            pltpu.VMEM((BLOCK, HALF), bf16),
            pltpu.VMEM((D,), f32),
            pltpu.VMEM((1, LAT_DEV), f32),
            pltpu.VMEM((PARTS, BLOCK, GROUP), bf16),
            pltpu.VMEM((BLOCK, D), bf16),
            pltpu.SemaphoreType.DMA((N_REMOTE,)),
            pltpu.SemaphoreType.DMA((N_REMOTE,)),
            pltpu.SemaphoreType.DMA((N_LOCAL,)),
            pltpu.SemaphoreType.REGULAR,
        ],
        cost_estimate=pl.CostEstimate(flops=90_000_000_000, bytes_accessed=10_000_000, transcendentals=0),
        compiler_params=pltpu.CompilerParams(
            collective_id=0, has_side_effects=True, vmem_limit_bytes=54 * 1024 * 1024
        ),
    )(resid, terms, dec_bias, enc_weight, enc_bias, dec_weight)


TILES = D // TILE


def adam_kernel(
    kept, first, second,
    weight_new, first_new, second_new, error_new,
    cen_in, slopes_in, weight_in, one_in, two_in, error_in, weight_out, one_out, two_out,
    in_sems, out_sems, lone_sems,
):
    def tile(t):
        return pl.ds(t * TILE, TILE)

    load_slopes = pltpu.make_async_copy(
        kept.at[pl.ds(D, ROWS), pl.ds(0, LAT_DEV)], slopes_in, lone_sems.at[0]
    )
    load_slopes.start()
    loads = []
    for t in range(TILES):
        pairs = (
            (kept.at[tile(t)], cen_in),
            (kept.at[pl.ds(D + t * TILE, TILE), pl.ds(LAT_DEV, LAT_DEV)], weight_in),
            (first.at[tile(t)], one_in),
            (second.at[tile(t)], two_in),
        )
        step = [
            pltpu.make_async_copy(src, dst.at[tile(t)], in_sems.at[i, t])
            for i, (src, dst) in enumerate(pairs)
        ]
        for copy in step:
            copy.start()
        loads.append(step)
    load_error = [
        pltpu.make_async_copy(
            kept.at[pl.ds(2 * D + i * BLOCK, BLOCK), pl.ds(0, 768)],
            error_in.at[:, pl.ds(i * 768, 768)],
            lone_sems.at[1 + i],
        )
        for i in range(3)
    ]
    for copy in load_error:
        copy.start()
    load_slopes.wait()
    corr_one = 1.0 - beta_one**STEP
    corr_two = 1.0 - beta_two**STEP
    stores = []
    for t in range(TILES):
        for copy in loads[t]:
            copy.wait()
        rows = tile(t)
        grad = jnp.dot(cen_in[rows], slopes_in[...], preferred_element_type=jnp.float32)
        one = beta_one * one_in[rows] + (1.0 - beta_one) * grad
        two = beta_two * two_in[rows] + (1.0 - beta_two) * grad * grad
        one_out[rows] = one
        two_out[rows] = two
        scaled = two * (1.0 / corr_two)
        change = one * (learn_rate / corr_one) / (scaled * lax.rsqrt(scaled) + adam_eps)
        weight_out[rows] = (weight_in[rows].astype(jnp.float32) - change).astype(jnp.bfloat16)
        pairs = ((one_out, first_new), (two_out, second_new), (weight_out, weight_new))
        for i, (src, dst) in enumerate(pairs):
            copy = pltpu.make_async_copy(src.at[rows], dst.at[rows], out_sems.at[i, t])
            copy.start()
            stores.append(copy)
    for copy in load_error:
        copy.wait()
    error_new[...] = error_in[:8, :]
    for copy in stores:
        copy.wait()


def adam(kept, first, second):
    bf16, f32 = jnp.bfloat16, jnp.float32
    anywhere = pl.BlockSpec(memory_space=pl.ANY)
    hbm = pl.BlockSpec(memory_space=pltpu.HBM)
    return pl.pallas_call(
        adam_kernel,
        out_shape=(
            jax.ShapeDtypeStruct((D, LAT_DEV), bf16),
            jax.ShapeDtypeStruct((D, LAT_DEV), f32),
            jax.ShapeDtypeStruct((D, LAT_DEV), f32),
            jax.ShapeDtypeStruct((8, D), bf16),
        ),
        in_specs=[anywhere] * 3,
        out_specs=(hbm, hbm, hbm, pl.BlockSpec(memory_space=pltpu.VMEM)),
        scratch_shapes=[
            pltpu.VMEM((D, ROWS), bf16),
            pltpu.VMEM((ROWS, LAT_DEV), bf16),
            pltpu.VMEM((D, LAT_DEV), bf16),
            pltpu.VMEM((D, LAT_DEV), f32),
            pltpu.VMEM((D, LAT_DEV), f32),
            pltpu.VMEM((BLOCK, D), bf16),
            pltpu.VMEM((D, LAT_DEV), bf16),
            pltpu.VMEM((D, LAT_DEV), f32),
            pltpu.VMEM((D, LAT_DEV), f32),
            pltpu.SemaphoreType.DMA((4, TILES)),
            pltpu.SemaphoreType.DMA((3, TILES)),
            pltpu.SemaphoreType.DMA((4,)),
        ],
        cost_estimate=pl.CostEstimate(
            flops=2 * ROWS * D * LAT_DEV, bytes_accessed=29_000_000, transcendentals=0
        ),
        compiler_params=pltpu.CompilerParams(vmem_limit_bytes=44 * 1024 * 1024),
    )(kept, first, second)


def on_device(
    resid_in, layer_terms, dec_bias, enc_weight, enc_bias, dec_weight, first_moment, second_moment
):
    kept = exchange(
        resid_in, layer_terms, dec_bias, enc_weight, enc_bias[None], dec_weight
    )
    return adam(kept, first_moment, second_moment)


def solution(mesh):
    in_specs = (
        P("lat", None),
        P("mp", "lat", None),
        P(),
        P(None, ("mp", "lat")),
        P(("mp", "lat")),
        P(("mp", "lat"), None),
        P(None, ("mp", "lat")),
        P(None, ("mp", "lat")),
    )
    out_specs = (
        P(None, ("mp", "lat")),
        P(None, ("mp", "lat")),
        P(None, ("mp", "lat")),
        P(("mp", "lat"), None),
    )
    return jax.shard_map(
        on_device, mesh=mesh, in_specs=in_specs, out_specs=out_specs, check_vma=False
    )
```

profile of v0, /device:TPU:1, one launch (start us, length us, event | category | flops | bytes accessed | tf_op | source)
XLA Modules:
  0.0 87.4 jit_solution(14580504086181090635)
XLA Ops:
  0.6 0.0 copy-start
  0.6 0.0 copy-start.1
  0.7 76.9 %shard_map.111.kept = bf16[8192,1024]{1,0:T(8,128)(2,1)} custom-call(bf16[32,2304]{1,0:T(8,128)(2,1)} %resid.1, bf16[1,32,2304]{2,1,0:T(8,128)(2,1)} %terms.1, f32[2304]{0:T(1024)} %dec_bias.1, bf16[2304,512]{1,0:T(8,128)(2,1)} %enc_weight.1, f32[1,512]{1,0:T(1,128)} %bitcast.1, bf16[512,2304]{1,0:T(8,128)(2,1)} %dec_weight.1), custom_call_target="tpu_custom_call" | custom-call | flops 89999998976 | bytes 10000000 | tf_op jit(solution)/shard_map/pallas_call | solution.py:425
  77.5 0.0 copy-done
  77.5 0.0 copy-done.1
  77.6 9.7 %shard_map.112 = (bf16[2304,512]{1,0:T(8,128)(2,1)}, f32[2304,512]{1,0:T(8,128)}, f32[2304,512]{1,0:T(8,128)}, bf16[8,2304]{1,0:T(8,128)(2,1)}) custom-call(bf16[8192,1024]{1,0:T(8,128)(2,1)} %shard_map.111.kept, f32[2304,512]{1,0:T(8,128)S(1)} %copy-done, f32[2304,512]{1,0:T(8,128)S(1)} %copy-done.1), custom_call_target="tpu_custom_call" | custom-call | flops 2415919104 | bytes 29000000 | tf_op jit(solution)/shard_map/pallas_call | solution.py:542
Async XLA Ops:
  0.6 76.9 %copy-start = (f32[2304,512]{1,0:T(8,128)S(1)}, f32[2304,512]{1,0:T(8,128)}, u32[]{:S(2)}) copy-start(f32[2304,512]{1,0:T(8,128)} %first.1) | copy-start | bytes 14155780
  0.6 76.9 %copy-start.1 = (f32[2304,512]{1,0:T(8,128)S(1)}, f32[2304,512]{1,0:T(8,128)}, u32[]{:S(2)}) copy-start(f32[2304,512]{1,0:T(8,128)} %second.1) | copy-start | bytes 14155780
where the time goes:
time: 87.5 us; the launch traced here: 87.4 us
  Pallas kernels  86.5 us (99%)
    pallas_call x1, Pallas kernels, exchange(): pl.pallas_call(exchange_kernel, out_shape=jax.ShapeDtypeStruct((KEPT, ROW...  76.9 us
    pallas_call x1, Pallas kernels, adam(): pl.pallas_call(adam_kernel, out_shape=(jax.ShapeDtypeStruct((D, LAT_DEV),...  9.68 us

commit v1 on v0

--- a/solution.py
+++ b/solution.py
@@ -212,9 +212,9 @@
             over(p, 1)
             over(p, 3)
         for p in range(PARTS):
-            for r, copy in ((0, four[p][0][0]), (1, three[p][2][1]), (3, four[p][1][3]), (2, three[p][2][2])):
+            for copy in (four[p][0][0], three[p][2][1], four[p][1][3], three[p][2][2]):
                 copy.wait_recv()
-                across.append(share(p, plane(p, 2, r), other))
+            over(p, 2)
         return across
 
     def nothing():
@@ -413,7 +413,7 @@
         copy.wait_send()
 
 
-N_REMOTE = 3 + 2 * PARTS * (15 + 10 + 2 + 7) + 4 + PARTS * (4 + 8 + 15)
+N_REMOTE = 3 + 2 * PARTS * (15 + 10 + 2 + 4) + 4 + PARTS * (4 + 8 + 15)
 N_LOCAL = 4 + 2 + 1 + 1 + 1 + 4 + 3
 KEPT = 8192
 
@@ -466,7 +466,8 @@
     )(resid, terms, dec_bias, enc_weight, enc_bias, dec_weight)
 
 
-TILES = D // TILE
+STEP_ROWS = 384
+TILES = D // STEP_ROWS
 
 
 def adam_kernel(
@@ -476,7 +477,7 @@
     in_sems, out_sems, lone_sems,
 ):
     def tile(t):
-        return pl.ds(t * TILE, TILE)
+        return pl.ds(t * STEP_ROWS, STEP_ROWS)
 
     load_slopes = pltpu.make_async_copy(
         kept.at[pl.ds(D, ROWS), pl.ds(0, LAT_DEV)], slopes_in, lone_sems.at[0]
@@ -486,7 +487,7 @@
     for t in range(TILES):
         pairs = (
             (kept.at[tile(t)], cen_in),
-            (kept.at[pl.ds(D + t * TILE, TILE), pl.ds(LAT_DEV, LAT_DEV)], weight_in),
+            (kept.at[pl.ds(D + t * STEP_ROWS, STEP_ROWS), pl.ds(LAT_DEV, LAT_DEV)], weight_in),
             (first.at[tile(t)], one_in),
             (second.at[tile(t)], two_in),
         )

time: 87.5 us -> 86.8 us (level)
  no operation moved by 1% of the time
where the time goes in v1:
time: 86.8 us; the launch traced here: 86.7 us
  Pallas kernels  85.8 us (99%)
    pallas_call x1, Pallas kernels, exchange(): pl.pallas_call(exchange_kernel, out_shape=jax.ShapeDtypeStruct((KEPT, ROW...  76.5 us
    pallas_call x1, Pallas kernels, adam(): pl.pallas_call(adam_kernel, out_shape=(jax.ShapeDtypeStruct((D, LAT_DEV),...  9.31 us

profile of v1, /device:TPU:1, one launch (start us, length us, event | category | flops | bytes accessed | tf_op | source)
XLA Modules:
  0.0 86.7 jit_solution(3319739106477153657)
XLA Ops:
  0.6 0.0 copy-start
  0.6 0.0 copy-start.1
  0.7 76.5 %shard_map.111.kept = bf16[8192,1024]{1,0:T(8,128)(2,1)} custom-call(bf16[32,2304]{1,0:T(8,128)(2,1)} %resid.1, bf16[1,32,2304]{2,1,0:T(8,128)(2,1)} %terms.1, f32[2304]{0:T(1024)} %dec_bias.1, bf16[2304,512]{1,0:T(8,128)(2,1)} %enc_weight.1, f32[1,512]{1,0:T(1,128)} %bitcast.1, bf16[512,2304]{1,0:T(8,128)(2,1)} %dec_weight.1), custom_call_target="tpu_custom_call" | custom-call | flops 89999998976 | bytes 10000000 | tf_op jit(solution)/shard_map/pallas_call | solution.py:425
  77.2 0.0 copy-done
  77.2 0.0 copy-done.1
  77.2 9.3 %shard_map.112 = (bf16[2304,512]{1,0:T(8,128)(2,1)}, f32[2304,512]{1,0:T(8,128)}, f32[2304,512]{1,0:T(8,128)}, bf16[8,2304]{1,0:T(8,128)(2,1)}) custom-call(bf16[8192,1024]{1,0:T(8,128)(2,1)} %shard_map.111.kept, f32[2304,512]{1,0:T(8,128)S(1)} %copy-done, f32[2304,512]{1,0:T(8,128)S(1)} %copy-done.1), custom_call_target="tpu_custom_call" | custom-call | flops 2415919104 | bytes 29000000 | tf_op jit(solution)/shard_map/pallas_call | solution.py:543
Async XLA Ops:
  0.6 76.6 %copy-start = (f32[2304,512]{1,0:T(8,128)S(1)}, f32[2304,512]{1,0:T(8,128)}, u32[]{:S(2)}) copy-start(f32[2304,512]{1,0:T(8,128)} %first.1) | copy-start | bytes 14155780
  0.6 76.6 %copy-start.1 = (f32[2304,512]{1,0:T(8,128)S(1)}, f32[2304,512]{1,0:T(8,128)}, u32[]{:S(2)}) copy-start(f32[2304,512]{1,0:T(8,128)} %second.1) | copy-start | bytes 14155780

commit v2 on v1

--- a/solution.py
+++ b/solution.py
@@ -18,6 +18,7 @@
 HALF = D // 2
 GROUP = HALF // 3
 PARTS = 3
+PIECES = 2
 LAT_DEV = 512
 ROWS = 1024
 BLOCK = 16
@@ -29,7 +30,7 @@
     resid, terms, dec_bias, enc_weight, enc_bias, dec_weight,
     kept_out,
     cen, err, cen_t, weight, dec, dec_t, norms, codes, cross_send, cross_recv, part_sum,
-    a_send, a_recv, b_send, b_recv, c_send, c_recv, plane_sum, slopes, half_sum,
+    b_send, b_recv, c_send, c_recv, plane_sum, slopes, half_sum,
     term_in, resid_in, bias_in, enc_bias_in, own_cen, error_rows,
     send_sems, recv_sems, local_sems, ready,
 ):
@@ -307,50 +308,27 @@
                     cen[g, t].reshape(TILE, GROUP).T
                 )
 
-    step_a = [{} for _ in range(PARTS)]
-    step_b = [[{}, {}] for _ in range(PARTS)]
-
-    def to_far(p, r, k):
-        a_send[p, r] = here(p, plane(p, 2, r)).astype(jnp.bfloat16)
-        step_a[p][r] = remote(a_send.at[p, r], a_recv.at[p, r], peer(ORDER[p][2], k))
-
-    def to_owner(p, way, r):
-        k = (1, 3)[way]
-        value = here(p, plane(p, k, r))
-        if r in ROUTE[way]:
-            step_a[p][r].wait_recv()
-            value = value + a_recv[p, r].astype(jnp.float32)
-        b_send[p, way, r] = value.astype(jnp.bfloat16)
-        step_b[p][way][r] = remote(b_send.at[p, way, r], b_recv.at[p, way, r], peer(ORDER[p][2], k))
-
-    for way, k in ((0, 1), (1, 3)):
-        for r in ROUTE[way]:
+    slots = (2, 1, 3, 0)
+    step_a = [[{} for _ in range(PIECES)] for _ in range(PARTS)]
+    width = 4 // PIECES
+    for piece in range(PIECES):
+        inside = pl.ds(piece * width, width)
+        for way, k in enumerate((2, 1, 3)):
             for p in range(PARTS):
-                to_far(p, r, k)
-    for r in (2, 1):
-        for p in range(PARTS):
-            to_far(p, r, 2)
-            for way in range(2):
-                to_owner(p, way, r)
-    for way in range(2):
-        for r in ROUTE[1 - way]:
-            for p in range(PARTS):
-                to_owner(p, way, r)
-    for way in range(2):
-        for r in ROUTE[way]:
-            for p in range(PARTS):
-                to_owner(p, way, r)
+                for slot in range(piece * width, (piece + 1) * width):
+                    b_send[p, way, slot] = here(p, plane(p, k, slots[slot])).astype(jnp.bfloat16)
+                step_a[p][piece][way] = remote(
+                    b_send.at[p, way, inside], b_recv.at[p, way, inside], peer(ORDER[p][2], k)
+                )
     turn_centered(0, 4)
     step_c = [{} for _ in range(PARTS)]
-    for r in (2, 1, 3, 0):
+    for slot, r in enumerate(slots):
         for p in range(PARTS):
             value = here(p, plane(p, 0, r))
-            if r in STRAIGHT:
-                step_a[p][r].wait_recv()
-                value = value + a_recv[p, r].astype(jnp.float32)
-            for way in range(2):
-                step_b[p][way][r].wait_recv()
-                value = value + b_recv[p, way, r].astype(jnp.float32)
+            for way in range(3):
+                if slot % width == 0:
+                    step_a[p][slot // width][way].wait_recv()
+                value = value + b_recv[p, way, slot].astype(jnp.float32)
             c_send[p, r] = value.astype(jnp.bfloat16).reshape(4, BLOCK, GROUP)
             if r == 0:
                 plane_sum[p] = value.reshape(4, BLOCK, GROUP)
@@ -413,7 +391,7 @@
         copy.wait_send()
 
 
-N_REMOTE = 3 + 2 * PARTS * (15 + 10 + 2 + 4) + 4 + PARTS * (4 + 8 + 15)
+N_REMOTE = 3 + 2 * PARTS * (15 + 10 + 2 + 4) + 4 + PARTS * (3 * PIECES + 15)
 N_LOCAL = 4 + 2 + 1 + 1 + 1 + 4 + 3
 KEPT = 8192
 
@@ -439,10 +417,8 @@
             pltpu.VMEM((PARTS, 4, 4, 64, GROUP), bf16),
             pltpu.VMEM((PARTS, 4, 4, 64, GROUP), bf16),
             pltpu.VMEM((PARTS, 4, 4, 64, GROUP), f32),
-            pltpu.VMEM((PARTS, 4, 64, GROUP), bf16),
-            pltpu.VMEM((PARTS, 4, 64, GROUP), bf16),
-            pltpu.VMEM((PARTS, 2, 4, 64, GROUP), bf16),
-            pltpu.VMEM((PARTS, 2, 4, 64, GROUP), bf16),
+            pltpu.VMEM((PARTS, 3, 4, 64, GROUP), bf16),
+            pltpu.VMEM((PARTS, 3, 4, 64, GROUP), bf16),
             pltpu.VMEM((PARTS, 4, 4, BLOCK, GROUP), bf16),
             pltpu.VMEM((PARTS, 4, 4, BLOCK, GROUP), bf16),
             pltpu.VMEM((PARTS, 4, BLOCK, GROUP), f32),

time: 86.8 us -> 88.6 us (1.021)
  Pallas kernels: 85.8 us -> 87.7 us
    pallas_call x1, Pallas kernels: 76.5 us -> 78.4 us  [exchange(): pl.pallas_call(exchange_kernel, out_shape=jax.ShapeDtypeStruct((KEPT, ROW...]
where the time goes in v2:
time: 88.6 us; the launch traced here: 88.5 us
  Pallas kernels  87.7 us (99%)
    pallas_call x1, Pallas kernels, exchange(): pl.pallas_call(exchange_kernel, out_shape=jax.ShapeDtypeStruct((KEPT, ROW...  78.4 us
    pallas_call x1, Pallas kernels, adam(): pl.pallas_call(adam_kernel, out_shape=(jax.ShapeDtypeStruct((D, LAT_DEV),...  9.31 us

profile of v2, /device:TPU:1, one launch (start us, length us, event | category | flops | bytes accessed | tf_op | source)
XLA Modules:
  0.0 88.5 jit_solution(7301054458213784240)
XLA Ops:
  0.6 0.0 copy-start
  0.6 0.0 copy-start.1
  0.7 78.4 %shard_map.111.kept = bf16[8192,1024]{1,0:T(8,128)(2,1)} custom-call(bf16[32,2304]{1,0:T(8,128)(2,1)} %resid.1, bf16[1,32,2304]{2,1,0:T(8,128)(2,1)} %terms.1, f32[2304]{0:T(1024)} %dec_bias.1, bf16[2304,512]{1,0:T(8,128)(2,1)} %enc_weight.1, f32[1,512]{1,0:T(1,128)} %bitcast.1, bf16[512,2304]{1,0:T(8,128)(2,1)} %dec_weight.1), custom_call_target="tpu_custom_call" | custom-call | flops 89999998976 | bytes 10000000 | tf_op jit(solution)/shard_map/pallas_call | solution.py:403
  79.0 0.0 copy-done
  79.0 0.0 copy-done.1
  79.0 9.3 %shard_map.112 = (bf16[2304,512]{1,0:T(8,128)(2,1)}, f32[2304,512]{1,0:T(8,128)}, f32[2304,512]{1,0:T(8,128)}, bf16[8,2304]{1,0:T(8,128)(2,1)}) custom-call(bf16[8192,1024]{1,0:T(8,128)(2,1)} %shard_map.111.kept, f32[2304,512]{1,0:T(8,128)S(1)} %copy-done, f32[2304,512]{1,0:T(8,128)S(1)} %copy-done.1), custom_call_target="tpu_custom_call" | custom-call | flops 2415919104 | bytes 29000000 | tf_op jit(solution)/shard_map/pallas_call | solution.py:519
Async XLA Ops:
  0.6 78.4 %copy-start = (f32[2304,512]{1,0:T(8,128)S(1)}, f32[2304,512]{1,0:T(8,128)}, u32[]{:S(2)}) copy-start(f32[2304,512]{1,0:T(8,128)} %first.1) | copy-start | bytes 14155780
  0.6 78.4 %copy-start.1 = (f32[2304,512]{1,0:T(8,128)S(1)}, f32[2304,512]{1,0:T(8,128)}, u32[]{:S(2)}) copy-start(f32[2304,512]{1,0:T(8,128)} %second.1) | copy-start | bytes 14155780
